TPU v7x, 256 devices: a whole 4x4x8 slice. The times are simulated.
256 devices in a mesh: wide: 32 (over z_hi, x, y), narrow: 8 (over z_lo, core).
Axes of the slice: x: 4, y: 4, z: 8 (z_hi: 2, z_lo: 4; z = z_hi * 4 + z_lo), core: 2. Of those that a mesh axis runs over, the one named last changes fastest.
Arguments:
- aux_vectors: float32 [4096, 8192], P('narrow', 'wide'), may hold values from -0.6 to 0.6
- occ_index: int32 [4096], P('narrow'), may hold values from 0 to 199
- vir_index: int32 [4096], P('narrow'), may hold values from 0 to 1999
- occ_energy: float32 [200], replicated, may hold values from -1.5 to -0.3
- vir_energy: float32 [2000], replicated, may hold values from 0.1 to 3
- frequency: float32 [1], replicated, may hold values from 0.2 to 2
Outputs:
- polar: float32 [8192, 8192], P('wide', 'narrow')
All inputs are finite; a program needn't handle non-finite values.
Results may differ from a plain program's by a relative error of at most 0.000055.
Values sent between devices are 32-bit elements; how exact they have to be, the bound alone decides.
A program may use at most 128 MiB of HBM per device.

v0:
```python
import jax
import jax.numpy as jnp
from jax import lax
from jax.sharding import PartitionSpec as P


def lookup(indices, table):
    columns = jnp.arange(table.shape[0], dtype=jnp.int32)
    return jnp.sum(jnp.where(indices[:, None] == columns[None, :], table[None, :], 0.0), axis=1)


def inner_product(left_rows, right_rows):
    return lax.dot_general(
        left_rows,
        right_rows,
        (((0,), (0,)), ((), ())),
        precision=lax.Precision.HIGHEST,
        preferred_element_type=jnp.float32,
    )


def shards(aux_vectors, occ_index, vir_index, occ_energy, vir_energy, frequency):
    gap = lookup(vir_index, vir_energy) - lookup(occ_index, occ_energy)
    omega = frequency[0]
    weights = 2.0 * gap / (gap * gap + omega * omega)
    scaled = aux_vectors * weights[:, None]
    products = inner_product(scaled, lax.all_gather(aux_vectors, "wide", axis=1, tiled=True))
    return lax.psum_scatter(products, "narrow", scatter_dimension=1, tiled=True)


def solution(mesh):
    return jax.shard_map(
        shards,
        mesh=mesh,
        in_specs=(P("narrow", "wide"), P("narrow"), P("narrow"), P(), P(), P()),
        out_specs=P("wide", "narrow"),
        check_vma=False,
    )
```

profile of v0, /device:TPU:65, one launch (start us, length us, event | category | flops | bytes accessed | tf_op | source)
XLA Modules:
  0.0 407.5 jit_solution(566357581367715290)
XLA Ops:
  6.5 0.0 all-gather.2.cloned.1.call-start
  6.5 0.7 all-gather.2.cloned.1.call-update
  7.3 0.0 reduce-scatter.2.cloned.1.call-start
  7.9 0.8 select_reduce_fusion.1
  8.8 1.2 select_reduce_fusion
  10.0 272.6 %all-gather.2.cloned.1.call-done = f32[512,8192]{1,0:T(8,128)} async-done(((f32[512,256]{1,0:T(8,128)}), f32[512,8192]{1,0:T(8,128)}) %all-gather.2.cloned.1.call-update) | async-done | bytes 16777232 | tf_op jit(solution)/shard_map/all_gather | solution.py:27
  282.6 20.0 %fusion = f32[256,8192]{1,0:T(8,128)} fusion(f32[512,8192]{1,0:T(8,128)} %all-gather.2.cloned.1.call-done, f32[512,256]{1,0:T(8,128)} %param.6, f32[512]{0:T(512)S(1)} %add_divide_fusion), kind=kOutput, calls=%fused_computation.2 | convolution fusion | flops 12885032960 | bytes 25692160 | tf_op jit(solution)/shard_map/dot_general | solution.py:13
  302.6 0.0 reduce-scatter.2.cloned.1.call-update
  302.7 98.0 %reduce-scatter.2.cloned.1.call-done = f32[256,1024]{1,0:T(8,128)} async-done(((f32[256,8192]{1,0:T(8,128)}), f32[256,1024]{1,0:T(8,128)}) %reduce-scatter.2.cloned.1.call-update) | async-done | bytes 1048592 | tf_op jit(solution)/shard_map/reduce_scatter | solution.py:28
  (1 shorter events, 0.0 us)
Async XLA Ops:
  6.5 276.1 %all-gather.2.cloned.1.call-start = ((), (), s32[]{:S(2)}) async-start(), calls=%async_computation.1 | async-start | bytes 17301504 | tf_op jit(solution)/shard_map/all_gather | solution.py:27
  7.3 393.4 %reduce-scatter.2.cloned.1.call-start = ((), (), s32[]{:S(2)}) async-start(), calls=%async_computation.2 | async-start | bytes 9437184 | tf_op jit(solution)/shard_map/reduce_scatter | solution.py:28
Sparse Core Ops, SparseCore 0:
  10.6 271.9 all-gather.1
  302.8 97.8 reduce-scatter.1
where the time goes:
time: 410 us; the launch traced here: 408 us
  waiting for transfers between devices  371 us (90%)
  matrix products  20 us (5%)
  between operations  14.1 us (3%)
    all_gather x1, waiting for transfers between devices, shards(): lax.all_gather(aux_vectors, 'wide', axis=1, tiled=True)  273 us
    reduce_scatter x1, waiting for transfers between devices, shards(): return lax.psum_scatter(products, 'narrow', scatter_dimension=1, tiled=True)  98 us
    dot_general x1, matrix products, inner_product(): lax.dot_general(left_rows, right_rows, (((0,), (0,)), ((), ())), precisio...  20 us
  transfers between devices with their start and end apart: 2, of which 2 were waited for; matrix products, arithmetic and copies ran while one was open for 1% of the time, Pallas kernels for 0%

commit v1 on v0

v1 whole, which is shorter than its diff:
```python
import jax
import jax.numpy as jnp
from jax import lax
from jax.experimental import pallas as pl
from jax.experimental.pallas import tpu as pltpu
from jax.sharding import PartitionSpec as P

MESH = pl.DeviceIdType.MESH
F32, BF16 = jnp.float32, jnp.bfloat16


def lookup(indices, table):
    columns = jnp.arange(table.shape[0], dtype=jnp.int32)
    return jnp.sum(jnp.where(indices[:, None] == columns[None, :], table[None, :], 0.0), axis=1)


def kernel(a_ref, w_ref, out_ref, G, J, W, RH, RL, acc, other, land,
           zs, zr, ws, wr, s1s, s1r, s2s, s2r, s3s, s3r, ds, dr, as_, ar):
    wide, narrow = lax.axis_index("wide"), lax.axis_index("narrow")
    zh, x, y = wide // 16, (wide // 4) % 4, wide % 4
    zl, c = narrow // 2, narrow % 2
    pos = zh * 4 + zl
    h, pi = zl % 2, zl // 2
    is_src = (x + y) % 2 == pi
    i_own, j_own = x // 2, y // 2

    def at(x_=x, y_=y, pos_=pos, c_=c):
        return ((pos_ // 4) * 16 + x_ * 4 + y_, (pos_ % 4) * 2 + c_)

    def remote(src, dst, send, recv, device):
        return pltpu.make_async_remote_copy(
            src_ref=src, dst_ref=dst, send_sem=send, recv_sem=recv, device_id=device, device_id_type=MESH)

    xs = [(x + d) % 4 for d in range(4)]
    ys = [(y + d) % 4 for d in range(4)]

    barrier = pltpu.get_barrier_semaphore()
    friends = [at(x_=xs[d]) for d in (1, 2, 3)] + [at(y_=ys[d]) for d in (1, 2, 3)]
    friends += [at(pos_=(pos + d) % 8) for d in range(1, 8)] + [at(c_=1 - c)]
    for device in friends:
        pl.semaphore_signal(barrier, inc=1, device_id=device, device_id_type=MESH)
    G[pos, 0] = a_ref[0:256, :]
    G[pos, 1] = a_ref[256:512, :]
    W[zl] = w_ref[...]
    pl.semaphore_wait(barrier, len(friends))

    def z_copy(way, d, half):
        q = (pos + 8 + (-d if way == 0 else d)) % 8
        to = (pos + (1 if way == 0 else 7)) % 8
        block = G.at[q, half]
        return remote(block, block, zs.at[way, d, half], zr.at[way, d, half], at(pos_=to))

    def z_wait(way, d, half):
        q = (pos + 8 + (-d if way == 0 else d)) % 8
        block = G.at[q, half]
        remote(block, block, zs.at[way, d - 1, half], zr.at[way, d - 1, half], at(pos_=(pos + 1) % 8)).wait_recv()

    def w_copy(t):
        return remote(W.at[zl], W.at[zl], ws.at[t], wr.at[zl], at(pos_=zh * 4 + (zl + t) % 4))

    def first(zq, half, t):
        d = (1, 3, 2)[t]
        piece = J.at[zq, y, i_own, half]
        if half == 0:
            return remote(piece, piece, s1s.at[zq, half, t], s1r.at[zq, half, i_own], at(x_=xs[d]))
        return remote(piece, piece, s1s.at[zq, half, t], s1r.at[zq, half, j_own], at(y_=ys[d]))

    def piece_of(zq, half, shift, k):
        if half == 0:
            return J.at[zq, ys[shift], k, half]
        return J.at[zq, 2 * k + (pi + xs[shift]) % 2, xs[shift] // 2, half]

    def neighbour(half, shift):
        return at(y_=ys[shift]) if half == 0 else at(x_=xs[shift])

    def second(zq, half, way, k):
        piece = piece_of(zq, half, 0, k)
        return remote(piece, piece, s2s.at[zq, half, way, k], s2r.at[zq, half, way, k],
                      neighbour(half, 1 if way == 0 else 3))

    def second_wait(zq, half, way, k):
        piece = piece_of(zq, half, 3 if way == 0 else 1, k)
        remote(piece, piece, s2s.at[zq, half, way, k], s2r.at[zq, half, way, k], neighbour(half, 1)).wait_recv()

    def third(zq, half, way):
        piece = piece_of(zq, half, 3 if way == 0 else 1, way)
        return remote(piece, piece, s3s.at[zq, half, way], s3r.at[zq, half, way],
                      neighbour(half, 1 if way == 0 else 3))

    def third_wait(zq, half, way):
        piece = piece_of(zq, half, 2, way)
        remote(piece, piece, s3s.at[zq, half, way], s3r.at[zq, half, way], neighbour(half, 1)).wait_recv()

    def stage1(zq, half):
        @pl.when(is_src)
        def _():
            block = G[zh * 4 + zq, half]
            J[zq, y, i_own, half] = jnp.where(h == 0, block[:, :128], block[:, 128:])
            for t in range(3):
                first(zq, half, t).start()

    def stage2(zq, half):
        own = i_own if half == 0 else j_own
        for k in range(2):
            @pl.when(jnp.logical_not(jnp.logical_and(is_src, own == k)))
            def _(k=k):
                piece = piece_of(zq, half, 0, k)
                remote(piece, piece, s1s.at[zq, half, 0], s1r.at[zq, half, k], neighbour(half, 1)).wait_recv()

            for way in range(2):
                second(zq, half, way, k).start()

    def stage3(zq, half):
        for way in range(2):
            second_wait(zq, half, way, way)
            third(zq, half, way).start()

    def stage4(zq, half):
        for way in range(2):
            second_wait(zq, half, way, 1 - way)
            third_wait(zq, half, way)

    def prepare(q, half):
        zq, zhq = q % 4, q // 4
        t = G[q, half].T * W[zq, 0:1, half * 256:half * 256 + 256]
        hi = t.astype(BF16)
        RH[zq, zhq, :, half * 256:half * 256 + 256] = hi
        RL[zq, zhq, :, half * 256:half * 256 + 256] = (t - hi.astype(F32)).astype(BF16)

    def unit(zq, zh1, order=lambda s: s, after=None):
        def body(s, carry):
            y2 = order(s)
            rows = [jnp.concatenate([J[zq, y2, 0, half], J[zq, y2, 1, half]], axis=1) for half in range(2)]
            b = jnp.concatenate(rows, axis=0)
            bh = b.astype(BF16)
            bl = (b - bh.astype(F32)).astype(BF16)
            ah, al = RH[zq, zh1], RL[zq, zh1]
            acc[y2, zh1] += (jnp.dot(ah, bh, preferred_element_type=F32)
                             + jnp.dot(ah, bl, preferred_element_type=F32)
                             + jnp.dot(al, bh, preferred_element_type=F32))
            return carry
        lax.fori_loop(0, 4, body, 0)

    for half in range(2):
        for way in range(2):
            z_copy(way, 0, half).start()
    for t in range(1, 4):
        w_copy(t).start()
    for half in range(2):
        stage1(zl, half)
    acc[...] = jnp.zeros_like(acc)
    for half in range(2):
        prepare(pos, half)
    for half in range(2):
        stage2(zl, half)
    for t in range(1, 4):
        zq = (zl + t) % 4
        remote(W.at[zq], W.at[zq], ws.at[t], wr.at[zq], at(pos_=zh * 4 + zq)).wait_recv()

    def own(d, do):
        if d == 0:
            do(zl)
            return
        for way in range(2):
            zq = zl - d if way == 0 else zl + d
            @pl.when(zq >= 0 if way == 0 else zq <= 3)
            def _(zq=zq):
                do(zq)

    for d in range(1, 5):
        for half in range(2):
            for way in range(2):
                if d == 4 and way != half:
                    continue
                z_wait(way, d, half)
                if d < 3 or (d == 3 and way == half):
                    z_copy(way, d, half).start()
                if d < 4:
                    zq = zl - d if way == 0 else zl + d
                    @pl.when(zq >= 0 if way == 0 else zq <= 3)
                    def _(zq=zq, half=half):
                        stage1(zq, half)
        own(d - 1, lambda zq: [stage3(zq, half) for half in range(2)])
        for half in range(2):
            if d < 4:
                prepare((pos + 8 - d) % 8, half)
                prepare((pos + d) % 8, half)
            else:
                prepare((pos + 4) % 8, half)
        if d < 4:
            own(d, lambda zq: [stage2(zq, half) for half in range(2)])
            own(d - 1, lambda zq: [stage4(zq, half) for half in range(2)])
            own(d - 1, lambda zq: unit(zq, zh))

    def far(zq):
        return jnp.logical_or(zq - zl == 3, zl - zq == 3)

    def rest(zq, carry):
        @pl.when(jnp.logical_not(far(zq)))
        def _():
            unit(zq, 1 - zh)
        return carry

    lax.fori_loop(0, 4, rest, 0)
    yc, yo = (pi + c) % 2, (pi + 1 - c) % 2

    def last(zq):
        for half in range(2):
            stage4(zq, half)
        for zh1 in range(2):
            unit(zq, zh1)

    own(3, last)

    def d_copy(k):
        return remote(acc.at[2 * k + yo], other.at[k], ds.at[k], dr.at[k], at(c_=1 - c))

    for k in range(2):
        d_copy(k).start()

    def a_copy(k, zh1, i):
        y2 = 2 * k + yc
        return remote(acc.at[y2, zh1, :, pl.ds(i * 128, 128)], land.at[y2, h],
                      as_.at[k, zh1, i], ar.at[zl, k], at(pos_=zh1 * 4 + 2 * zh + i))

    def each_out(do, do_self):
        for k in range(2):
            yield_k = k
            for zh1 in range(2):
                for i in range(2):
                    mine = zh1 * 4 + 2 * zh + i == pos

                    @pl.when(jnp.logical_not(mine))
                    def _(zh1=zh1, i=i, k=k):
                        do(k, zh1, i)

                    if do_self is not None:
                        @pl.when(mine)
                        def _(zh1=zh1, i=i, k=k):
                            do_self(k, zh1, i)

    for k in range(2):
        d_copy(k).wait_recv()
        acc[2 * k + yc] += other[k]

    def keep(k, zh1, i):
        land[2 * k + yc, h] = acc[2 * k + yc, zh1, :, i * 128:i * 128 + 128]

    each_out(lambda k, zh1, i: a_copy(k, zh1, i).start(), keep)

    for k in range(2):
        for zs_ in range(4):
            @pl.when((zl // 2) * 4 + zs_ != pos)
            def _(zs_=zs_, k=k):
                y2 = 2 * k + (zs_ // 2 + c) % 2
                block = land.at[y2, zs_ % 2]
                remote(block, block, as_.at[0, 0, 0], ar.at[zs_, k], at(c_=1 - c)).wait_recv()
    for y2 in range(4):
        for hh in range(2):
            out_ref[:, y2 * 256 + hh * 128:y2 * 256 + hh * 128 + 128] = land[y2, hh]

    for way in range(2):
        for half in range(2):
            for d in range(4):
                if d < 3 or way == half:
                    z_copy(way, d, half).wait_send()
    for t in range(1, 4):
        w_copy(t).wait_send()

    def sent(zq, carry):
        for half in range(2):
            @pl.when(is_src)
            def _(half=half):
                for t in range(3):
                    first(zq, half, t).wait_send()
            for way in range(2):
                for k in range(2):
                    second(zq, half, way, k).wait_send()
                third(zq, half, way).wait_send()
        return carry

    lax.fori_loop(0, 4, sent, 0)
    for k in range(2):
        d_copy(k).wait_send()
    each_out(lambda k, zh1, i: a_copy(k, zh1, i).wait_send(), None)


def shards(aux_vectors, occ_index, vir_index, occ_energy, vir_energy, frequency):
    gap = lookup(vir_index, vir_energy) - lookup(occ_index, occ_energy)
    omega = frequency[0]
    weights = 2.0 * gap / (gap * gap + omega * omega)
    weights = jnp.broadcast_to(weights[None, :], (8, 512))
    dma = pltpu.SemaphoreType.DMA
    return pl.pallas_call(
        kernel,
        out_shape=jax.ShapeDtypeStruct((256, 1024), F32),
        in_specs=[pl.BlockSpec(memory_space=pltpu.VMEM)] * 2,
        out_specs=pl.BlockSpec(memory_space=pltpu.VMEM),
        scratch_shapes=[
            pltpu.VMEM((8, 2, 256, 256), F32),
            pltpu.VMEM((4, 4, 2, 2, 256, 128), F32),
            pltpu.VMEM((4, 8, 512), F32),
            pltpu.VMEM((4, 2, 256, 512), BF16),
            pltpu.VMEM((4, 2, 256, 512), BF16),
            pltpu.VMEM((4, 2, 256, 256), F32),
            pltpu.VMEM((2, 2, 256, 256), F32),
            pltpu.VMEM((4, 2, 256, 128), F32),
            dma((2, 4, 2)), dma((2, 4, 2)),
            dma((4,)), dma((4,)),
            dma((4, 2, 3)), dma((4, 2, 2)),
            dma((4, 2, 2, 2)), dma((4, 2, 2, 2)),
            dma((4, 2, 2)), dma((4, 2, 2)),
            dma((2,)), dma((2,)),
            dma((2, 2, 2)), dma((4, 2)),
        ],
        compiler_params=pltpu.CompilerParams(
            collective_id=0, has_side_effects=True, vmem_limit_bytes=48 * 2**20),
        cost_estimate=pl.CostEstimate(flops=2 * 3 * 512 * 1024 * 2048, bytes_accessed=2 * 2**20, transcendentals=0),
        name="gather_multiply",
    )(aux_vectors, weights)


def solution(mesh):
    return jax.shard_map(
        shards,
        mesh=mesh,
        in_specs=(P("narrow", "wide"), P("narrow"), P("narrow"), P(), P(), P()),
        out_specs=P("wide", "narrow"),
        check_vma=False,
    )
```

time: 410 us -> 118 us (0.29)
  waiting for transfers between devices: 371 us -> 0 us
  Pallas kernels: 0 us -> 112 us
  matrix products: 20 us -> 0 us
  between operations: 14.1 us -> 0.69 us
    all_gather x1 -> x0, waiting for transfers between devices: 273 us -> none  [shards(): lax.all_gather(aux_vectors, 'wide', axis=1, tiled=True)]
    pallas_call x0 -> x1, Pallas kernels: none -> 112 us  [shards(): pl.pallas_call(kernel, out_shape=jax.ShapeDtypeStruct((256, 1024), F32),...]
    reduce_scatter x1 -> x0, waiting for transfers between devices: 98 us -> none  [shards(): return lax.psum_scatter(products, 'narrow', scatter_dimension=1, tiled=True)]
    dot_general x1 -> x0, matrix products: 20 us -> none  [inner_product(): lax.dot_general(left_rows, right_rows, (((0,), (0,)), ((), ())), precisio...]
  transfers between devices with their start and end apart: 2 -> 0, of which waited for: 2 -> 0; matrix products, arithmetic and copies ran while one was open for 1% -> 0% of each run, Pallas kernels for 0% -> 0%
where the time goes in v1:
time: 118 us; the launch traced here: 116 us
  Pallas kernels  112 us (95%)
  other arithmetic  2.08 us (2%)
  local copies, waits for them, and re-layouts  2.01 us (2%)
    pallas_call x1, Pallas kernels, shards(): pl.pallas_call(kernel, out_shape=jax.ShapeDtypeStruct((256, 1024), F32),...  112 us

profile of v1, /device:TPU:65, one launch (start us, length us, event | category | flops | bytes accessed | tf_op | source)
XLA Modules:
  0.0 116.5 jit_solution(3828099374131440910)
XLA Ops:
  0.7 0.8 select_reduce_fusion.1
  1.5 1.2 %select_reduce_fusion = f32[512]{0:T(512)S(1)} fusion(f32[2000]{0:T(1024)} %param.10, s32[512]{0:T(512)} %param.8), kind=kLoop, calls=%fused_computation | loop fusion | flops 3071488 | bytes 12096 | tf_op jit(solution)/shard_map/reduce_sum | solution.py:14
  2.8 0.0 copy-start
  2.8 1.0 copy-done
  3.8 111.7 %gather_multiply.1 = f32[256,1024]{1,0:T(8,128)S(1)} custom-call(f32[512,256]{1,0:T(8,128)S(1)} %copy-done, f32[8,512]{1,0:T(8,128)S(1)} %broadcast_in_dim.40.w_ref), custom_call_target="tpu_custom_call" | custom-call | flops 6442450944 | bytes 2097152 | tf_op jit(solution)/shard_map/gather_multiply/pallas_call | solution.py:294
  115.5 1.0 copy.9
  (2 shorter events, 0.0 us)
Async XLA Ops:
  2.8 1.0 copy-start

commit v2 on v0

v2 whole, which is shorter than its diff:
```python
import jax
import jax.numpy as jnp
from jax import lax
from jax.experimental import pallas as pl
from jax.experimental.pallas import tpu as pltpu
from jax.sharding import PartitionSpec as P

MESH = pl.DeviceIdType.MESH
F32, BF16 = jnp.float32, jnp.bfloat16


def lookup(indices, table_ref, quarter, found):
    size = table_ref.shape[0] // 4

    def body(j, found):
        for k in range(10):
            at = quarter * size + j * 10 + k
            found = jnp.where(indices == at, table_ref[at], found)
        return found
    return lax.fori_loop(0, size // 10, body, found)


def kernel(a_ref, occ_index, vir_index, occ_table, vir_table, omega_ref, out_ref, G, J, W, R, acc, other, land,
           zs, zr, ws, wr, s1s, s1r, s2s, s2r, s3s, s3r, ds, dr, as_, ar, ls, os, levels, relay, br, bs,
           occ_ref, vir_ref, occ_energy, vir_energy, frequency, ts):
    wide, narrow = lax.axis_index("wide"), lax.axis_index("narrow")
    zh, x, y = wide // 16, (wide // 4) % 4, wide % 4
    zl, c = narrow // 2, narrow % 2
    pos = zh * 4 + zl
    h, pi = zl // 2, zl % 2

    def at(x_=x, y_=y, pos_=pos, c_=c):
        return ((pos_ // 4) * 16 + x_ * 4 + y_, (pos_ % 4) * 2 + c_)

    def remote(src, dst, send, recv, device):
        return pltpu.make_async_remote_copy(
            src_ref=src, dst_ref=dst, send_sem=send, recv_sem=recv, device_id=device, device_id_type=MESH)

    xs = [(x + d) % 4 for d in range(4)]
    ys = [(y + d) % 4 for d in range(4)]
    step = jnp.where(zl < 2, 1, 3)
    turn = [(zl + t * step) % 4 for t in range(4)]

    barrier = pltpu.get_barrier_semaphore()
    friends = [at(x_=xs[d]) for d in (1, 2, 3)] + [at(y_=ys[d]) for d in (1, 2, 3)]
    friends += [at(pos_=(pos + d) % 8) for d in range(1, 8)] + [at(c_=1 - c)]
    for device in friends:
        pl.semaphore_signal(barrier, inc=1, device_id=device, device_id_type=MESH)

    def load(hh, r):
        return pltpu.make_async_copy(
            a_ref.at[pl.ds(r * 256, 256), pl.ds(hh * 128, 128)], G.at[pos, hh, r], ls.at[hh, r])

    for hh in range(2):
        for r in range(2):
            load(hh, r).start()
    tables = [pltpu.make_async_copy(src, dst, ts.at[n]) for n, (src, dst) in enumerate((
        (occ_index, occ_ref), (vir_index, vir_ref), (occ_table, occ_energy), (vir_table, vir_energy),
        (omega_ref, frequency)))]
    for table in tables:
        table.start()
    pl.semaphore_wait(barrier, len(friends))
    for hh in range(2):
        for r in range(2):
            load(hh, r).wait()

    CHUNKS = [(d, o, r) for o in range(2) for d in (1, 2, 3) for r in range(2)] + [(4, 0, 0), (4, 0, 1)]

    def z_block(way, d, o, r):
        return G.at[(pos + 8 + (-d if way == 0 else d)) % 8, o if way == 1 else 1 - o, r]

    def z_copy(way, d, o, r):
        block = z_block(way, d, o, r)
        return remote(block, block, zs.at[way, d, o, r], zr.at[way, d, o, r],
                      at(pos_=(pos + (1 if way == 0 else 7)) % 8))

    def z_wait(way, d, o, r):
        block = z_block(way, d, o, r)
        remote(block, block, zs.at[way, d - 1, o, r], zr.at[way, d - 1, o, r], at(pos_=(pos + 1) % 8)).wait_recv()

    def z_sent(d, o):
        return d < 3 or o == 0

    def w_copy(t):
        return remote(W.at[zl], W.at[zl], ws.at[t], wr.at[zl], at(pos_=zh * 4 + (zl + t) % 4))

    def line(r, shift):
        return at(x_=xs[shift]) if r == 0 else at(y_=ys[shift])

    def cross(r, shift):
        return at(y_=ys[shift]) if r == 0 else at(x_=xs[shift])

    def behind(s, r):
        return (x - y - pi - 2 * s + 16) % 4 if r == 0 else (y - x + pi + 2 * s) % 4

    def piece(t, s, r, shift):
        y2 = ys[shift] if r == 0 else (xs[shift] - pi - 2 * s + 8) % 4
        return J.at[turn[t], s, y2, r]

    def first(t, s, r, way):
        p = piece(t, s, r, 0)
        return remote(p, p, s1s.at[t, s, r, way], s1r.at[t, s, r], line(r, 1 if way == 0 else 3))

    def second(t, s, r, way):
        p = piece(t, s, r, 0)
        return remote(p, p, s2s.at[t, s, r, way], s2r.at[t, s, r, way], cross(r, 1 if way == 0 else 3))

    def second_wait(t, s, r, way):
        p = piece(t, s, r, 3 if way == 0 else 1)
        remote(p, p, s2s.at[t, s, r, way], s2r.at[t, s, r, way], cross(r, 1)).wait_recv()

    def third(t, s, r):
        way = (t + r) % 2
        p = piece(t, s, r, 3 if way == 0 else 1)
        return remote(p, p, s3s.at[t, s, r], s3r.at[t, s, r], cross(r, 1 if way == 0 else 3))

    def third_wait(t, s, r):
        p = piece(t, s, r, 2)
        remote(p, p, s3s.at[t, s, r], s3r.at[t, s, r], cross(r, 1)).wait_recv()

    def stage1(t, s, r):
        @pl.when(behind(s, r) == 0)
        def _():
            J[turn[t], s, y, r] = G[zh * 4 + turn[t], h, r]
            for way in range(2):
                first(t, s, r, way).start()

    def stage2(t, s, r):
        @pl.when(behind(s, r) != 0)
        def _():
            p = piece(t, s, r, 0)
            remote(p, p, s1s.at[t, s, r, 0], s1r.at[t, s, r], line(r, 1)).wait_recv()

        way = (t + r) % 2

        @pl.when(behind(s, r) == (1 if way == 0 else 3))
        def _():
            first(t, s, r, way).start()

        for w in range(2):
            second(t, s, r, w).start()

    def stage3(t, s, r):
        second_wait(t, s, r, (t + r) % 2)
        third(t, s, r).start()

    def stage4(t, s, r):
        second_wait(t, s, r, 1 - (t + r) % 2)
        third_wait(t, s, r)

    def prepare(q, hh, r):
        zq, zhq = q % 4, q // 4
        w = jnp.concatenate([W[zq, 2 * r:2 * r + 1], W[zq, 2 * r + 1:2 * r + 2]], axis=1)
        v = G[q, hh, r].T * w
        hi = v.astype(BF16)
        rows = pl.ds(pl.multiple_of(hh * 128, 128), 128)
        R[zq, zhq, 0, rows, r * 256:r * 256 + 256] = hi
        R[zq, zhq, 1, rows, r * 256:r * 256 + 256] = (v - hi.astype(F32)).astype(BF16)

    def unit(t, s, zh1):
        zq = turn[t]

        def body(p, carry):
            rows = [jnp.concatenate([J[zq, s, p, r], J[zq, s, p + 2, r]], axis=1) for r in range(2)]
            b = jnp.concatenate(rows, axis=0)
            bh = b.astype(BF16)
            bl = (b - bh.astype(F32)).astype(BF16)
            both = jnp.dot(R[zq, zh1].reshape(512, 512), bh, preferred_element_type=F32)
            acc[s, p, zh1] += both[:256] + both[256:] + jnp.dot(R[zq, zh1, 0], bl, preferred_element_type=F32)
            return carry
        lax.fori_loop(0, 2, body, 0)

    yc = (pi + c) % 2

    def rows_of(e):
        return 1 - zh if e == 0 else zh

    def d_copy(s, e):
        zh1 = rows_of(e)
        return remote(acc.at[s, 1 - yc, zh1], other.at[s, zh1], ds.at[s, e], dr.at[s, e], at(c_=1 - c))

    def goes_to(s, k, e):
        i = ((2 * k + yc + pi + 2 * s) % 4) // 2
        return rows_of(e) * 4 + 2 * zh + i

    def detour(q):
        return jnp.logical_or(jnp.logical_and(pos == 0, q == 4), jnp.logical_and(pos == 7, q == 3))

    def result(s, k, e):
        return acc.at[s, yc, rows_of(e), :, pl.ds(k * 128, 128)]

    def a_copy(s, k, e):
        return remote(result(s, k, e), land.at[2 * k + yc, h],
                      as_.at[s, k, e], ar.at[zl, k], at(pos_=goes_to(s, k, e)))

    def b_copy(s, k):
        return remote(result(s, k, 0), relay.at[s], as_.at[s, k, 0], br.at[s],
                      at(pos_=jnp.where(pos == 0, 6, 1)))

    def c_copy(s):
        zq, i = jnp.where(pos == 6, 0, 3), jnp.where(pos == 6, 0, 1)
        ycq = (zq % 2 + c) % 2
        k = (i + 2 - ((ycq + zq % 2 + 2 * s) % 4) // 2) % 2
        return remote(relay.at[s], land.at[2 * k + ycq, zq // 2], bs.at[s], ar.at[zq, k],
                      at(pos_=jnp.where(pos == 6, 4, 3)))

    passes = jnp.logical_or(pos == 6, pos == 1)

    def send_out(s, e):
        for k in range(2):
            q = goes_to(s, k, e)

            @pl.when(jnp.logical_and(q != pos, jnp.logical_not(detour(q))))
            def _(k=k):
                a_copy(s, k, e).start()

            if e == 0:
                @pl.when(detour(q))
                def _(k=k):
                    b_copy(s, k).start()
            else:
                @pl.when(q == pos)
                def _(k=k):
                    land[2 * k + yc, h] = acc[s, yc, zh, :, k * 128:k * 128 + 128]

    def pass_on(s):
        @pl.when(passes)
        def _():
            remote(relay.at[s], relay.at[s], bs.at[s], br.at[s], at(c_=1 - c)).wait_recv()
            c_copy(s).start()

    def arrive(n, way):
        d, o, r = CHUNKS[n]
        z_wait(way, d, o, r)
        if d < 3:
            z_copy(way, d, o, r).start()

    def launch(d, o):
        for way in range(2):
            for r in range(2):
                z_copy(way, d, o, r).start()

    def ready(n):
        d, o, r = CHUNKS[n]
        for way in range(2):
            prepare((pos + 8 + (-d if way == 0 else d)) % 8, o if way == 1 else 1 - o, r)

    launch(0, 0)

    def weigh(quarter):
        if quarter == 0:
            levels[...] = jnp.zeros_like(levels)
            for table in tables:
                table.wait()
        levels[0] = lookup(vir_ref[...], vir_energy, quarter, levels[0])
        levels[1] = lookup(occ_ref[...], occ_energy, quarter, levels[1])
        if quarter < 3:
            return
        gap = levels[0] - levels[1]
        omega = frequency[0]
        weights = 2.0 * gap / (gap * gap + omega * omega)
        W[zl] = jnp.concatenate([weights, weights], axis=0)
        for t in range(1, 4):
            w_copy(t).start()

    def begin():
        acc[...] = jnp.zeros_like(acc)
        for t in range(1, 4):
            zq = (zl + t) % 4
            remote(W.at[zq], W.at[zq], ws.at[t], wr.at[zq], at(pos_=zh * 4 + zq)).wait_recv()
        for hh in range(2):
            for r in range(2):
                prepare(pos, hh, r)

    def own(t, s):
        unit(t, s, zh)

    def far(t, s):
        unit(t, s, 1 - zh)

    PLAN = (
        "1001 1011 1000 z00",
        "z01 1100 2011 1010",
        "1110 z11 z10 1101",
        "w0 2100 z21 z20",
        "1111 1210 2001 1200",
        "z31 z30 1211 y",
        "1201 2101 w1 w2",
        "w3 2000 z40 z41",
        "c p2 2200 z50",
        "3001 z51 z61 p1",
        "z60 1310 1300 2201",
        "z71 z70 1301 1311",
        "3000 2211 4001 2300",
        "z81 3100 z80 2301",
        "z91 z90 p9 2310",
        "3101 x 3201 2311",
        "p8 za1 3200 3300",
        "2210 3301 p3 p5",
        "za0 p4 4000 2110",
        "p6 u00 p0 zb1",
        "zc1 4101 4100 p7",
        "u10 zb0 zc0 pb",
        "pa v10 pc 4201",
        "zd1 4200 v20 zd0",
        "pd v00 2010 4300",
        "3310 4301 v30 u30",
        "d00 u20 d01 3011",
        "3311 3211 2111 3210",
        "o00 o01 3010 3110",
        "4310 4311 v31 4211",
        "3111 4210 v21 u21",
        "4011 u31 4010 u01",
        "v01 4110 4111 u11",
        "r0 v11 d10 d11",
        "o10 o11 r1",
    )
    for token in [word for words in PLAN for word in words.split()]:
        kind, args = token[0], [int(v, 16) for v in token[1:]]
        if kind == "z":
            arrive(*args)
        elif kind == "y":
            launch(0, 1)
        elif kind == "x":
            launch(3, 0)
        elif kind == "w":
            weigh(*args)
        elif kind == "c":
            begin()
        elif kind == "p":
            ready(args[0])
        elif kind in "1234":
            {"1": stage1, "2": stage2, "3": stage3, "4": stage4}[kind](*args)
        elif kind == "u":
            own(*args)
        elif kind == "v":
            far(*args)
        elif kind == "d":
            d_copy(*args).start()
        elif kind == "o":
            s, e = args
            d_copy(s, e).wait_recv()
            acc[s, yc, rows_of(e)] += other[s, rows_of(e)]
            send_out(s, e)
        elif kind == "r":
            pass_on(*args)

    def put(zq, k):
        y2, hh = 2 * k + (zq % 2 + c) % 2, zq // 2
        columns = pl.ds(pl.multiple_of(y2 * 256 + hh * 128, 128), 128)
        return pltpu.make_async_copy(land.at[y2, hh], out_ref.at[:, columns], os.at[zq, k])

    def part(zq, s):
        return (((2 * (zl % 2) + c - (zq % 2 + c) % 2 - zq % 2 + 4) % 4) // 2 + s) % 2

    for s in range(2):
        for zq in range(4):
            k = part(zq, s)

            @pl.when((zl // 2) * 4 + zq != pos)
            def _(zq=zq, k=k):
                block = land.at[2 * k + (zq % 2 + c) % 2, zq // 2]
                remote(block, block, as_.at[0, 0, 0], ar.at[zq, k], at(c_=1 - c)).wait_recv()

            put(zq, k).start()
    for zq in range(4):
        for k in range(2):
            put(zq, k).wait()

    for way in range(2):
        for d in range(4):
            for o in range(2):
                for r in range(2):
                    if z_sent(d, o):
                        z_copy(way, d, o, r).wait_send()
    for t in range(1, 4):
        w_copy(t).wait_send()
    for s in range(2):
        for t in range(4):
            for r in range(2):
                fwd = (t + r) % 2
                for way in range(2):
                    sends = behind(s, r) == 0
                    if way == fwd:
                        sends = jnp.logical_or(sends, behind(s, r) == (1 if way == 0 else 3))

                    @pl.when(sends)
                    def _(t=t, s=s, r=r, way=way):
                        first(t, s, r, way).wait_send()

                    second(t, s, r, way).wait_send()
                third(t, s, r).wait_send()
        for e in range(2):
            d_copy(s, e).wait_send()
            for k in range(2):
                @pl.when(goes_to(s, k, e) != pos)
                def _(s=s, k=k, e=e):
                    a_copy(s, k, e).wait_send()

        @pl.when(passes)
        def _(s=s):
            c_copy(s).wait_send()


def shards(aux_vectors, occ_index, vir_index, occ_energy, vir_energy, frequency):
    dma = pltpu.SemaphoreType.DMA
    hbm = pl.BlockSpec(memory_space=pltpu.HBM)
    return pl.pallas_call(
        kernel,
        out_shape=jax.ShapeDtypeStruct((256, 1024), F32),
        in_specs=[hbm] * 6,
        out_specs=hbm,
        scratch_shapes=[
            pltpu.VMEM((8, 2, 2, 256, 128), F32),
            pltpu.VMEM((4, 2, 4, 2, 256, 128), F32),
            pltpu.VMEM((4, 8, 128), F32),
            pltpu.VMEM((4, 2, 2, 256, 512), BF16),
            pltpu.VMEM((2, 2, 2, 256, 256), F32),
            pltpu.VMEM((2, 2, 256, 256), F32),
            pltpu.VMEM((4, 2, 256, 128), F32),
            dma((2, 4, 2, 2)), dma((2, 4, 2, 2)),
            dma((4,)), dma((4,)),
            dma((4, 2, 2, 2)), dma((4, 2, 2)),
            dma((4, 2, 2, 2)), dma((4, 2, 2, 2)),
            dma((4, 2, 2)), dma((4, 2, 2)),
            dma((2, 2)), dma((2, 2)),
            dma((2, 2, 2)), dma((4, 2)),
            dma((2, 2)), dma((4, 2)),
            pltpu.VMEM((2, 4, 128), F32),
            pltpu.VMEM((2, 256, 128), F32), dma((2,)), dma((2,)),
            pltpu.VMEM((4, 128), jnp.int32), pltpu.VMEM((4, 128), jnp.int32),
            pltpu.SMEM((200,), F32), pltpu.SMEM((2000,), F32), pltpu.SMEM((1,), F32), dma((5,)),
        ],
        compiler_params=pltpu.CompilerParams(
            collective_id=0, has_side_effects=True, vmem_limit_bytes=63 * 2**20),
        cost_estimate=pl.CostEstimate(flops=2 * 3 * 512 * 1024 * 2048, bytes_accessed=2 * 2**20, transcendentals=0),
        name="gather_multiply",
    )(aux_vectors, occ_index.reshape(4, 128), vir_index.reshape(4, 128), occ_energy, vir_energy, frequency)


def solution(mesh):
    return jax.shard_map(
        shards,
        mesh=mesh,
        in_specs=(P("narrow", "wide"), P("narrow"), P("narrow"), P(), P(), P()),
        out_specs=P("wide", "narrow"),
        check_vma=False,
    )
```

time: 410 us -> 104 us (0.25)
  waiting for transfers between devices: 371 us -> 0 us
  Pallas kernels: 0 us -> 101 us
  matrix products: 20 us -> 0 us
  between operations: 14.1 us -> 0.66 us
    all_gather x1 -> x0, waiting for transfers between devices: 273 us -> none  [shards(): lax.all_gather(aux_vectors, 'wide', axis=1, tiled=True)]
    pallas_call x0 -> x1, Pallas kernels: none -> 101 us  [shards(): pl.pallas_call(kernel, out_shape=jax.ShapeDtypeStruct((256, 1024), F32),...]
    reduce_scatter x1 -> x0, waiting for transfers between devices: 98 us -> none  [shards(): return lax.psum_scatter(products, 'narrow', scatter_dimension=1, tiled=True)]
    dot_general x1 -> x0, matrix products: 20 us -> none  [inner_product(): lax.dot_general(left_rows, right_rows, (((0,), (0,)), ((), ())), precisio...]
  transfers between devices with their start and end apart: 2 -> 0, of which waited for: 2 -> 0; matrix products, arithmetic and copies ran while one was open for 1% -> 0% of each run, Pallas kernels for 0% -> 0%
where the time goes in v2:
time: 104 us
  Pallas kernels  101 us (97%)
  local copies, waits for them, and re-layouts  2.31 us (2%)
    pallas_call x1, Pallas kernels, shards(): pl.pallas_call(kernel, out_shape=jax.ShapeDtypeStruct((256, 1024), F32),...  101 us
    unnamed x1, local copies, waits for them, and re-layouts  2.31 us

profile of v2, /device:TPU:65, one launch (start us, length us, event | category | flops | bytes accessed | tf_op | source)
XLA Modules:
  0.0 104.2 jit_solution(10011228086032476321)
XLA Ops:
  0.7 101.2 %gather_multiply.1 = f32[256,1024]{1,0:T(8,128)} custom-call(f32[512,256]{1,0:T(8,128)} %a_ref.1, s32[4,128]{1,0:T(4,128)} %bitcast.2, s32[4,128]{1,0:T(4,128)} %bitcast.3, f32[200]{0:T(256)} %occ_table.1, f32[2000]{0:T(1024)} %vir_table.1, f32[1]{0:T(128)S(6)} %copy.8.omega_ref), custom_call_target="tpu_custom_call" | custom-call | flops 6442450944 | bytes 2097152 | tf_op jit(solution)/shard_map/gather_multiply/pallas_call | solution.py:408
  101.9 2.3 %copy.9 = f32[256,1024]{1,0:T(8,128)} copy(f32[256,1024]{1,0:T(8,128)} %gather_multiply.1) | data formatting | bytes 2097152

commit v3 on v2

--- a/solution.py
+++ b/solution.py
@@ -91,7 +91,7 @@
         return at(y_=ys[shift]) if r == 0 else at(x_=xs[shift])
 
     def behind(s, r):
-        return (x - y - pi - 2 * s + 16) % 4 if r == 0 else (y - x + pi + 2 * s) % 4
+        return (x - y - pi - 2 * s + 16) % 4 if r == 0 else (y - x + pi + 2 * s + 4) % 4
 
     def piece(t, s, r, shift):
         y2 = ys[shift] if r == 0 else (xs[shift] - pi - 2 * s + 8) % 4
@@ -160,15 +160,13 @@
     def unit(t, s, zh1):
         zq = turn[t]
 
-        def body(p, carry):
+        for p in range(2):
             rows = [jnp.concatenate([J[zq, s, p, r], J[zq, s, p + 2, r]], axis=1) for r in range(2)]
             b = jnp.concatenate(rows, axis=0)
             bh = b.astype(BF16)
             bl = (b - bh.astype(F32)).astype(BF16)
             both = jnp.dot(R[zq, zh1].reshape(512, 512), bh, preferred_element_type=F32)
             acc[s, p, zh1] += both[:256] + both[256:] + jnp.dot(R[zq, zh1, 0], bl, preferred_element_type=F32)
-            return carry
-        lax.fori_loop(0, 2, body, 0)
 
     yc = (pi + c) % 2
 
@@ -279,41 +277,41 @@
         unit(t, s, 1 - zh)
 
     PLAN = (
-        "1001 1011 1000 z00",
-        "z01 1100 2011 1010",
-        "1110 z11 z10 1101",
-        "w0 2100 z21 z20",
-        "1111 1210 2001 1200",
-        "z31 z30 1211 y",
-        "1201 2101 w1 w2",
-        "w3 2000 z40 z41",
-        "c p2 2200 z50",
-        "3001 z51 z61 p1",
-        "z60 1310 1300 2201",
-        "z71 z70 1301 1311",
-        "3000 2211 4001 2300",
-        "z81 3100 z80 2301",
-        "z91 z90 p9 2310",
-        "3101 x 3201 2311",
-        "p8 za1 3200 3300",
-        "2210 3301 p3 p5",
-        "za0 p4 4000 2110",
-        "p6 u00 p0 zb1",
-        "zc1 4101 4100 p7",
-        "u10 zb0 zc0 pb",
-        "pa v10 pc 4201",
-        "zd1 4200 v20 zd0",
-        "pd v00 2010 4300",
-        "3310 4301 v30 u30",
-        "d00 u20 d01 3011",
-        "3311 3211 2111 3210",
-        "o00 o01 3010 3110",
-        "4310 4311 v31 4211",
-        "3111 4210 v21 u21",
-        "4011 u31 4010 u01",
-        "v01 4110 4111 u11",
-        "r0 v11 d10 d11",
-        "o10 o11 r1",
+        "1001 w0 1000 w1",
+        "w2 w3 1010 c",
+        "z01 z00 1110 1100",
+        "z10 1011 z11 1101",
+        "1111 2000 z20 z21",
+        "1200 2110 1210 z30",
+        "z31 2100 1201 y",
+        "2101 2010 3000 z41",
+        "2001 1211 p1 z51",
+        "2200 z40 z50 p5",
+        "z61 z60 1300 1310",
+        "p6 2011 z70 z71",
+        "1311 p7 1301 2210",
+        "3101 2201 p0 2111",
+        "p3 3100 z81 z80",
+        "2300 z91 2310 3001",
+        "z90 p4 p9 p2",
+        "p8 x 4000 2301",
+        "3201 2311 3200 2211",
+        "3011 za1 za0 4100",
+        "zb0 3301 3300 zb1",
+        "pb 4001 3010 zc0",
+        "zd0 zc1 pc pa",
+        "zd1 4101 u10 v10",
+        "4201 pd v00 4200",
+        "v20 4300 4301 v30",
+        "d00 u30 3310 u20",
+        "o00 3311 u00 d01",
+        "3211 3210 3110 3111",
+        "4010 o01 4011 4310",
+        "v01 4311 v31 4211",
+        "4210 v21 r0 4110",
+        "4111 v11 d10 u01",
+        "u21 u31 o10 u11",
+        "d11 o11 r1",
     )
     for token in [word for words in PLAN for word in words.split()]:
         kind, args = token[0], [int(v, 16) for v in token[1:]]
@@ -345,28 +343,6 @@
         elif kind == "r":
             pass_on(*args)
 
-    def put(zq, k):
-        y2, hh = 2 * k + (zq % 2 + c) % 2, zq // 2
-        columns = pl.ds(pl.multiple_of(y2 * 256 + hh * 128, 128), 128)
-        return pltpu.make_async_copy(land.at[y2, hh], out_ref.at[:, columns], os.at[zq, k])
-
-    def part(zq, s):
-        return (((2 * (zl % 2) + c - (zq % 2 + c) % 2 - zq % 2 + 4) % 4) // 2 + s) % 2
-
-    for s in range(2):
-        for zq in range(4):
-            k = part(zq, s)
-
-            @pl.when((zl // 2) * 4 + zq != pos)
-            def _(zq=zq, k=k):
-                block = land.at[2 * k + (zq % 2 + c) % 2, zq // 2]
-                remote(block, block, as_.at[0, 0, 0], ar.at[zq, k], at(c_=1 - c)).wait_recv()
-
-            put(zq, k).start()
-    for zq in range(4):
-        for k in range(2):
-            put(zq, k).wait()
-
     for way in range(2):
         for d in range(4):
             for o in range(2):
@@ -390,6 +366,30 @@
 
                     second(t, s, r, way).wait_send()
                 third(t, s, r).wait_send()
+
+    def put(zq, k):
+        y2, hh = 2 * k + (zq % 2 + c) % 2, zq // 2
+        columns = pl.ds(pl.multiple_of(y2 * 256 + hh * 128, 128), 128)
+        return pltpu.make_async_copy(land.at[y2, hh], out_ref.at[:, columns], os.at[zq, k])
+
+    def part(zq, s):
+        return (((2 * (zl % 2) + c - (zq % 2 + c) % 2 - zq % 2 + 4) % 4) // 2 + s) % 2
+
+    for s in range(2):
+        for zq in range(4):
+            k = part(zq, s)
+
+            @pl.when((zl // 2) * 4 + zq != pos)
+            def _(zq=zq, k=k):
+                block = land.at[2 * k + (zq % 2 + c) % 2, zq // 2]
+                remote(block, block, as_.at[0, 0, 0], ar.at[zq, k], at(c_=1 - c)).wait_recv()
+
+            put(zq, k).start()
+    for zq in range(4):
+        for k in range(2):
+            put(zq, k).wait()
+
+    for s in range(2):
         for e in range(2):
             d_copy(s, e).wait_send()
             for k in range(2):
@@ -407,7 +407,7 @@
     hbm = pl.BlockSpec(memory_space=pltpu.HBM)
     return pl.pallas_call(
         kernel,
-        out_shape=jax.ShapeDtypeStruct((256, 1024), F32),
+        out_shape=pltpu.VMEM((256, 1024), F32),
         in_specs=[hbm] * 6,
         out_specs=hbm,
         scratch_shapes=[
@@ -432,7 +432,7 @@
             pltpu.SMEM((200,), F32), pltpu.SMEM((2000,), F32), pltpu.SMEM((1,), F32), dma((5,)),
         ],
         compiler_params=pltpu.CompilerParams(
-            collective_id=0, has_side_effects=True, vmem_limit_bytes=63 * 2**20),
+            collective_id=0, has_side_effects=True, vmem_limit_bytes=62 * 2**20),
         cost_estimate=pl.CostEstimate(flops=2 * 3 * 512 * 1024 * 2048, bytes_accessed=2 * 2**20, transcendentals=0),
         name="gather_multiply",
     )(aux_vectors, occ_index.reshape(4, 128), vir_index.reshape(4, 128), occ_energy, vir_energy, frequency)

time: 104 us -> 98.2 us (0.944)
  Pallas kernels: 101 us -> 96.5 us
  local copies, waits for them, and re-layouts: 2.31 us -> 0.97 us
    pallas_call x1, Pallas kernels: 101 us -> 96.5 us  [shards(): pl.pallas_call(kernel, out_shape=pltpu.VMEM((256, 1024), F32), in_specs=[...]
    unnamed x1, local copies, waits for them, and re-layouts: 2.31 us -> 0.97 us
where the time goes in v3:
time: 98.2 us; the launch traced here: 98.1 us
  Pallas kernels  96.5 us (98%)
    pallas_call x1, Pallas kernels, shards(): pl.pallas_call(kernel, out_shape=pltpu.VMEM((256, 1024), F32), in_specs=[...  96.5 us

profile of v3, /device:TPU:65, one launch (start us, length us, event | category | flops | bytes accessed | tf_op | source)
XLA Modules:
  0.0 98.1 jit_solution(7434722080946177495)
XLA Ops:
  0.7 96.5 %gather_multiply.1 = f32[256,1024]{1,0:T(8,128)S(1)} custom-call(f32[512,256]{1,0:T(8,128)} %a_ref.1, s32[4,128]{1,0:T(4,128)} %bitcast.2, s32[4,128]{1,0:T(4,128)} %bitcast.3, f32[200]{0:T(256)} %occ_table.1, f32[2000]{0:T(1024)} %vir_table.1, f32[1]{0:T(128)S(6)} %copy.9.omega_ref), custom_call_target="tpu_custom_call" | custom-call | flops 6442450944 | bytes 2097152 | tf_op jit(solution)/shard_map/gather_multiply/pallas_call | solution.py:408
  97.2 1.0 copy.8

commit v4 on v3

--- a/solution.py
+++ b/solution.py
@@ -42,7 +42,7 @@
     turn = [(zl + t * step) % 4 for t in range(4)]
 
     barrier = pltpu.get_barrier_semaphore()
-    friends = [at(x_=xs[d]) for d in (1, 2, 3)] + [at(y_=ys[d]) for d in (1, 2, 3)]
+    friends = [at(x_=xs[d]) for d in (1, 3)] + [at(y_=ys[d]) for d in (1, 3)]
     friends += [at(pos_=(pos + d) % 8) for d in range(1, 8)] + [at(c_=1 - c)]
     for device in friends:
         pl.semaphore_signal(barrier, inc=1, device_id=device, device_id_type=MESH)
@@ -303,8 +303,8 @@
         "zd1 4101 u10 v10",
         "4201 pd v00 4200",
         "v20 4300 4301 v30",
-        "d00 u30 3310 u20",
-        "o00 3311 u00 d01",
+        "d00 u30 u20 o00",
+        "3310 3311 u00 d01",
         "3211 3210 3110 3111",
         "4010 o01 4011 4310",
         "v01 4311 v31 4211",

time: 98.2 us -> 97.7 us (level)
  no operation moved by 1% of the time
where the time goes in v4:
time: 97.7 us
  Pallas kernels  96 us (98%)
    pallas_call x1, Pallas kernels, shards(): pl.pallas_call(kernel, out_shape=pltpu.VMEM((256, 1024), F32), in_specs=[...  96 us

profile of v4, /device:TPU:65, one launch (start us, length us, event | category | flops | bytes accessed | tf_op | source)
XLA Modules:
  0.0 97.7 jit_solution(5744858748086997029)
XLA Ops:
  0.7 96.0 %gather_multiply.1 = f32[256,1024]{1,0:T(8,128)S(1)} custom-call(f32[512,256]{1,0:T(8,128)} %a_ref.1, s32[4,128]{1,0:T(4,128)} %bitcast.2, s32[4,128]{1,0:T(4,128)} %bitcast.3, f32[200]{0:T(256)} %occ_table.1, f32[2000]{0:T(1024)} %vir_table.1, f32[1]{0:T(128)S(6)} %copy.9.omega_ref), custom_call_target="tpu_custom_call" | custom-call | flops 6442450944 | bytes 2097152 | tf_op jit(solution)/shard_map/gather_multiply/pallas_call | solution.py:408
  96.7 1.0 copy.8
